TPU v7x, 256 devices: a whole 4x4x8 slice. The times are simulated.
256 devices in a mesh: dp: 2 (over core), span: 8 (over z), head: 16 (over x, y).
Axes of the slice: x: 4, y: 4, z: 8, core: 2. Of those that a mesh axis runs over, the one named last changes fastest.
Arguments:
- hidden_in: bfloat16 [8192, 4096], P(('dp', 'span'), 'head'), parts along dimension 0, may hold values from -6 to 6
- norm_gain: bfloat16 [4096], P('head'), may hold values from 0.099609375 to 1.8984375
- w_query: bfloat16 [4096, 4096], P(None, 'head'), may hold values from -0.375 to 0.375
- enc_states: bfloat16 [32768, 1024], P(('dp', 'span', 'head')), parts along dimension 0
- w_key: bfloat16 [1024, 4096], P(None, 'head'), may hold values from -0.1875 to 0.1875
- w_value: bfloat16 [1024, 4096], P(None, 'head'), may hold values from -0.1875 to 0.1875
- w_out: bfloat16 [4096, 4096], P('head'), may hold values from -0.5 to 0.5
- block_counts: int32 [16], P('dp'), parts along dimension 0, may hold values from 1 to 16, as said below
Outputs:
- cross_out: bfloat16 [8192, 4096], P(('dp', 'span'), 'head'), parts along dimension 0
There are 2 independent parts, one for each index of `dp`. A program takes and returns all parts, laid end to end along the dimension named above; an argument that names none is the same for every part. Nothing has to cross between parts.
Inputs may be any that keep to these rules, and one draw needn't show every extreme that they name: block_counts[g] is the number of live blocks of group g: the first block_counts[g] of its 16 block slots hold encoder tokens, the rest are padding; in every draw some group has all 16 live.
All inputs are finite; a program needn't handle non-finite values.
Results may differ from a plain program's by a relative error of at most 0.023.
The roundings to bfloat16 on the way count: a program that leaves them out, or rounds other values in their place, can miss the bound.
Values may be sent and summed in bfloat16 or wider, within the bound.
A program may use at most 128 MiB of HBM per device.

v0:
```python
import math

import jax
import jax.numpy as jnp
from jax import lax
from jax.sharding import PartitionSpec as P

HD = 128


def fold_tiles(carry_state, query_heads, keys_values, is_live):
    key_total = keys_values.shape[1]
    tile_rows = math.gcd(key_total, 512)
    tile_count = key_total // tile_rows
    heads_local = query_heads.shape[1]
    scale = 1.0 / math.sqrt(HD)

    def tile_work(inner, key_block, live_block):
        running_max, running_sum, accumulator = inner
        key_heads = key_block[0].reshape(tile_rows, heads_local, HD)
        value_heads = key_block[1].reshape(tile_rows, heads_local, HD)
        scores = (
            jnp.einsum("qhd,khd->hqk", query_heads, key_heads, preferred_element_type=jnp.float32)
            * scale
        )
        masked = jnp.where(live_block[None, None, :], scores, -1e30)
        new_max = jnp.maximum(running_max, jnp.max(masked, axis=2))
        factor = jnp.exp(running_max - new_max)
        weights = jnp.where(live_block[None, None, :], jnp.exp(scores - new_max[:, :, None]), 0.0)
        running_sum = running_sum * factor + jnp.sum(weights, axis=2)
        update = jnp.einsum(
            "hqk,khd->qhd",
            weights.astype(jnp.bfloat16),
            value_heads,
            preferred_element_type=jnp.float32,
        )
        accumulator = accumulator * jnp.transpose(factor)[:, :, None] + update
        return (new_max, running_sum, accumulator)

    def one_tile(tile_index, inner):
        offset = tile_index * tile_rows
        key_block = lax.dynamic_slice_in_dim(keys_values, offset, tile_rows, 1)
        live_block = lax.dynamic_slice_in_dim(is_live, offset, tile_rows, 0)
        return tile_work(inner, key_block, live_block)

    return lax.fori_loop(0, tile_count, one_tile, carry_state)


def empty_state(query_count, heads_local):
    return (
        jnp.full((heads_local, query_count), -1e30, jnp.float32),
        jnp.zeros((heads_local, query_count), jnp.float32),
        jnp.zeros((query_count, heads_local, HD), jnp.float32),
    )


def per_device(hidden_in, norm_gain, w_query, enc_states, w_key, w_value, w_out, block_counts):
    full_rows, full_gain = (
        lax.all_gather(hidden_in, "head", axis=1, tiled=True),
        lax.all_gather(norm_gain, "head", axis=0, tiled=True),
    )
    row_values = full_rows.astype(jnp.float32)
    mean_square = jnp.mean(row_values * row_values, axis=1, keepdims=True)
    normed = (row_values * lax.rsqrt(mean_square + 1e-05) * full_gain.astype(jnp.float32)).astype(
        jnp.bfloat16
    )
    queries = jnp.dot(normed, w_query, preferred_element_type=jnp.float32).astype(jnp.bfloat16)
    local_rows = queries.shape[0]
    width_local = queries.shape[1]
    heads_local = width_local // HD
    block_rows = enc_states.shape[0]
    group_count = block_counts.shape[0]
    portion = lax.all_gather(enc_states, "head", axis=0, tiled=True)
    key_part = jnp.dot(portion, w_key, preferred_element_type=jnp.float32).astype(jnp.bfloat16)
    value_part = jnp.dot(portion, w_value, preferred_element_type=jnp.float32).astype(jnp.bfloat16)
    group_kv = jnp.stack([key_part, value_part])
    group_rows = group_kv.shape[1]
    group_ids = jnp.arange(group_count, dtype=jnp.int32)
    query_heads = queries.reshape(local_rows, heads_local, HD)
    portion = lax.all_gather(group_kv, "span", axis=1, tiled=True)
    row_index = jnp.arange(portion.shape[1], dtype=jnp.int32)
    group_of = row_index // group_rows
    live_limit = jnp.sum(
        jnp.where(group_of[:, None] == group_ids[None, :], block_counts[None, :], 0), axis=1
    )
    is_live = row_index % group_rows < live_limit * block_rows
    running_max, running_sum, accumulator = fold_tiles(
        empty_state(local_rows, heads_local), query_heads, portion, is_live
    )
    attended = accumulator / jnp.transpose(running_sum)[:, :, None]
    attended = attended.reshape(local_rows, width_local).astype(jnp.bfloat16)
    partial_out = jnp.dot(attended, w_out, preferred_element_type=jnp.float32)
    return lax.psum_scatter(
        partial_out.astype(jnp.bfloat16), "head", scatter_dimension=1, tiled=True
    )


def solution(mesh):
    placed = (
        P(("dp", "span"), "head"),
        P("head"),
        P(None, "head"),
        P(("dp", "span", "head"), None),
        P(None, "head"),
        P(None, "head"),
        P("head", None),
        P("dp"),
    )
    return jax.shard_map(
        per_device, mesh=mesh, in_specs=placed, out_specs=P(("dp", "span"), "head"), check_vma=False
    )
```

profile of v0, /device:TPU:2, one launch (start us, length us, event | category | flops | bytes accessed | tf_op | source)
XLA Modules:
  0.0 525.8 jit_solution(3555236409772667026)
XLA Ops:
  8.1 61.3 %all-gather.5.cloned.1.call-done = bf16[2048,1024]{1,0:T(8,128)(2,1)} async-done(((bf16[128,1024]{1,0:T(8,128)(2,1)}), bf16[2048,1024]{1,0:T(8,128)(2,1)}) %all-gather.5.cloned.1.call-update) | async-done | bytes 4194320 | tf_op jit(solution)/shard_map/all_gather | solution.py:73
  69.3 3.7 fusion.18
  73.0 1.3 fusion.17
  74.3 1.5 pad_maximum_fusion
  76.5 21.1 %all-gather = bf16[16,1,256]{2,1,0:T(2,128)(2,1)S(1)} all-gather(bf16[1,1,256]{2,1,0:T(2,128)(2,1)S(1)} %reshape.33), channel_id=1, replica_groups=mesh['dp'=2,'span'=8,'head'=16] {'head'}, dimensions={0}, use_global_device_ids=true | all-gather | bytes 8704 | tf_op jit(solution)/shard_map/all_gather | solution.py:60
  98.0 35.8 %all-gather.9.cloned.1.call-done = bf16[512,4096]{1,0:T(8,128)(2,1)} async-done(((bf16[512,256]{1,0:T(8,128)(2,1)}), bf16[512,4096]{1,0:T(8,128)(2,1)}) %all-gather.9.cloned.1.call-update) | async-done | bytes 4194320 | tf_op jit(solution)/shard_map/all_gather | solution.py:59
  133.8 3.2 fusion.10
  137.3 3.2 fusion.19
  140.6 167.5 %all-gather.7.cloned.1.call-done = bf16[2,16384,256]{2,1,0:T(8,128)(2,1)} async-done(((bf16[2,2048,256]{2,1,0:T(8,128)(2,1)}), bf16[2,16384,256]{2,1,0:T(8,128)(2,1)}) %all-gather.7.cloned.1.call-update) | async-done | bytes 16777232 | tf_op jit(solution)/shard_map/all_gather | solution.py:80
  308.1 125.6 %while.18 = (s32[]{:T(128)}, f32[2,512]{1,0:T(2,128)S(1)}, f32[2,512]{1,0:T(2,128)S(1)}, f32[512,2,128]{0,2,1:T(8,128)}, pred[16384]{0:T(1024)(128)(4,1)S(1)}, /...) while((s32[]{:T(128)}, f32[2,512]{1,0:T(2,128)S(1)}, ...), condition=%wide.region_5.6_spmd.clone, body=%wide.region_2.5_spmd.clone.sunk | while | flops 274601984 | bytes 14486279 | solution.py:46
  308.2 1.1 constant_dynamic-slice_fusion.3
  312.1 1.1 constant_dynamic-slice_fusion.3
  316.1 1.1 constant_dynamic-slice_fusion.3
  320.0 1.1 constant_dynamic-slice_fusion.3
  327.8 1.1 constant_dynamic-slice_fusion.3
  335.7 1.1 constant_dynamic-slice_fusion.3
  339.6 1.1 constant_dynamic-slice_fusion.3
  343.5 1.1 constant_dynamic-slice_fusion.3
  347.5 1.1 constant_dynamic-slice_fusion.3
  351.4 1.1 constant_dynamic-slice_fusion.3
  355.3 1.1 constant_dynamic-slice_fusion.3
  433.7 1.1 divide_convert_fusion
  434.8 3.2 convolution_convert_fusion
  438.1 81.2 %reduce-scatter.2.cloned.1.call-done = bf16[512,256]{1,0:T(8,128)(2,1)} async-done(((bf16[512,4096]{1,0:T(8,128)(2,1)}), bf16[512,256]{1,0:T(8,128)(2,1)}) %reduce-scatter.2.cloned.1.call-update) | async-done | bytes 262160 | tf_op jit(solution)/shard_map/reduce_scatter | solution.py:93
  (467 shorter events, 114.4 us)
Async XLA Ops:
  6.5 428.3 %copy-start = (bf16[256,4096]{1,0:T(8,128)(2,1)S(1)}, bf16[256,4096]{1,0:T(8,128)(2,1)}, u32[]{:S(2)}) copy-start(bf16[256,4096]{1,0:T(8,128)(2,1)} %param.16) | copy-start | bytes 6291460
  6.5 62.8 %all-gather.5.cloned.1.call-start = ((), (), s32[]{:S(2)}) async-start(), calls=%async_computation.1 | async-start | bytes 4456448 | tf_op jit(solution)/shard_map/all_gather | solution.py:73
  7.3 126.5 %all-gather.9.cloned.1.call-start = ((), (), s32[]{:S(2)}) async-start(), calls=%async_computation.3 | async-start | bytes 4456448 | tf_op jit(solution)/shard_map/all_gather | solution.py:59
  8.0 65.0 %copy-start.6 = (bf16[1024,256]{1,0:T(8,128)(2,1)S(1)}, bf16[1024,256]{1,0:T(8,128)(2,1)}, u32[]{:S(2)}) copy-start(bf16[1024,256]{1,0:T(8,128)(2,1)} %param.14) | copy-start | bytes 1572868
  8.0 300.1 %all-gather.7.cloned.1.call-start = ((), (), s32[]{:S(2)}) async-start(), calls=%async_computation.2 | async-start | bytes 18874368 | tf_op jit(solution)/shard_map/all_gather | solution.py:80
  69.3 3.7 copy-start.5
  75.8 21.8 %copy-start.4 = (s32[8]{0:T(128)S(1)}, s32[8]{0:T(128)}, u32[]{:S(2)}) copy-start(s32[8]{0:T(128)} %param.17) | copy-start | bytes 100
  75.9 443.4 %reduce-scatter.2.cloned.1.call-start = ((), (), s32[]{:S(2)}) async-start(), calls=%async_computation.4 | async-start | bytes 4456448 | tf_op jit(solution)/shard_map/reduce_scatter | solution.py:93
  133.8 3.4 copy-start.1
  309.6 1.0 copy-start.2
  313.5 1.0 copy-start.2
  317.4 1.0 copy-start.2
  325.3 1.0 copy-start.2
  333.1 1.0 copy-start.2
  341.0 1.0 copy-start.2
  348.8 1.0 copy-start.2
  356.7 1.0 copy-start.2
  364.5 1.0 copy-start.2
  368.4 1.0 copy-start.2
  372.4 1.0 copy-start.2
  376.3 1.0 copy-start.2
  384.1 1.0 copy-start.2
  392.0 1.0 copy-start.2
  399.8 1.0 copy-start.2
  (50 other events, 44.7 us)
Sparse Core Ops, SparseCore 0:
  9.8 59.4 all-gather.4
  71.7 62.0 all-gather.8
  135.6 172.4 all-gather.6
  438.2 81.0 reduce-scatter.1
where the time goes:
time: 528 us; the launch traced here: 526 us
  waiting for transfers between devices  347 us (66%)
  local copies, waits for them, and re-layouts  71.6 us (14%)
  matrix products  48.6 us (9%)
  other arithmetic  21.5 us (4%)
  blocking collectives  21.1 us (4%)
  between operations  13.2 us (2%)
    all_gather x1, waiting for transfers between devices, per_device(): portion = lax.all_gather(group_kv, 'span', axis=1, tiled=True)  168 us
    reduce_scatter x1, waiting for transfers between devices, per_device(): lax.psum_scatter(partial_out.astype(jnp.bfloat16), 'head', scatter_dimens...  81.2 us
    all_gather x1, waiting for transfers between devices, per_device(): portion = lax.all_gather(enc_states, 'head', axis=0, tiled=True)  61.3 us
    all_gather x1, waiting for transfers between devices, per_device(): lax.all_gather(hidden_in, 'head', axis=1, tiled=True)  35.8 us
    while x224, local copies, waits for them, and re-layouts  34.2 us
    slice x32, local copies, waits for them, and re-layouts, tile_work(): value_heads = key_block[1].reshape(tile_rows, heads_local, HD)  34 us
    all_gather x1, blocking collectives, per_device(): lax.all_gather(norm_gain, 'head', axis=0, tiled=True)  21.1 us
    dot_general x32, matrix products, tile_work(): jnp.einsum('hqk,khd->qhd', weights.astype(jnp.bfloat16), value_heads, pre...  19.4 us
  transfers between devices with their start and end apart: 4, of which 4 were waited for; matrix products, arithmetic and copies ran while one was open for 3% of the time, Pallas kernels for 0%

commit v1 on v0

v1 whole, which is shorter than its diff:
```python
import math

import jax
import jax.numpy as jnp
from jax import lax
from jax.experimental import pallas as pl
from jax.experimental.pallas import tpu as pltpu
from jax.sharding import PartitionSpec as P

HD = 128
X = 4
Y = 4
Z = 8
HEAD = X * Y
T = 256
CHUNKS = 2
F = 256
BLOCK = 128
SLOTS = 16
KEYS = BLOCK * SLOTS
DE = 1024
LOG2E = 1.4426950408889634
COEF = LOG2E / math.sqrt(HD)
NEG = -1e30
F32 = jnp.float32
BF16 = jnp.bfloat16
MESH = pl.DeviceIdType.MESH


def wrap(value, size):
    return lax.rem(value + 2 * size, size)


class Place:
    def __init__(self):
        self.dp = lax.axis_index("dp")
        self.z = lax.axis_index("span")
        self.head = lax.axis_index("head")
        self.x = lax.div(self.head, Y)
        self.y = lax.rem(self.head, Y)

    def slot(self, dx, dy):
        return wrap(self.x + dx, X) * Y + wrap(self.y + dy, Y)

    def at_xy(self, dx, dy):
        return (self.dp, self.z, self.slot(dx, dy))

    def at_z(self, dz):
        return (self.dp, wrap(self.z + dz, Z), self.head)


class Gather:
    REL = (0, -1, 1, 2)

    def __init__(self, place, buf, rows, send, recv):
        self.place, self.buf, self.rows, self.send, self.recv = place, buf, rows, send, recv
        self.started = []

    def shift(self, half, da, db):
        return (db, da) if half == 0 else (da, db)

    def part(self, half, da, db, quarter):
        base = half * (self.rows // 2)
        count = self.rows // 2
        if quarter is not None:
            count = self.rows // 4
            base = base + quarter * count
        return self.buf.at[self.place.slot(*self.shift(half, da, db)), pl.ds(base, count)]

    def copy(self, half, index, ref, to):
        return pltpu.make_async_remote_copy(
            src_ref=ref,
            dst_ref=ref,
            send_sem=self.send.at[half * 20 + index],
            recv_sem=self.recv.at[half * 20 + index],
            device_id=to,
            device_id_type=MESH,
        )

    def go(self, half, index, da, db, quarter, ta, tb):
        copy = self.copy(
            half,
            index,
            self.part(half, da, db, quarter),
            self.place.at_xy(*self.shift(half, ta, tb)),
        )
        copy.start()
        self.started.append(copy)

    def take(self, half, index, da, db, quarter):
        ref = self.part(half, da, db, quarter)
        self.copy(half, index, ref, self.place.at_xy(1, 0)).wait_recv()

    def line(self, half, which):
        base = 4 + 4 * which
        rel = self.REL[which]
        self.go(half, base, rel, 0, None, 0, 1)
        self.go(half, base + 1, rel, 0, None, 0, -1)

    def pass_on(self, half, which):
        base = 4 + 4 * which
        rel = self.REL[which]
        self.take(half, base, rel, -1, None)
        self.go(half, base + 2, rel, -1, 0, 0, 1)
        self.take(half, base + 1, rel, 1, None)
        self.go(half, base + 3, rel, 1, 1, 0, -1)

    def s0(self):
        for half in range(2):
            self.go(half, 0, 0, 0, None, 1, 0)
            self.go(half, 1, 0, 0, None, -1, 0)
        for half in range(2):
            self.line(half, 0)

    def s1(self):
        for half in range(2):
            self.take(half, 0, -1, 0, None)
            self.go(half, 2, -1, 0, 0, 1, 0)
            self.take(half, 1, 1, 0, None)
            self.go(half, 3, 1, 0, 1, -1, 0)
        for half in range(2):
            self.line(half, 1)
            self.line(half, 2)

    def s2(self):
        for half in range(2):
            self.pass_on(half, 0)

    def s3(self):
        for half in range(2):
            self.take(half, 2, 2, 0, 0)
            self.take(half, 3, 2, 0, 1)
            self.line(half, 3)

    def s4(self):
        for which in (1, 2):
            for half in range(2):
                self.pass_on(half, which)

    def s5(self):
        for half in range(2):
            self.pass_on(half, 3)

    def s6(self):
        for which in range(4):
            for half in range(2):
                base = 4 + 4 * which
                rel = self.REL[which]
                self.take(half, base + 2, rel, 2, 0)
                self.take(half, base + 3, rel, 2, 1)

    def finish(self):
        for copy in self.started:
            copy.wait_send()


class QueryRing:
    def __init__(self, place, buf, chunk, send, recv):
        self.place, self.buf, self.chunk, self.send, self.recv = place, buf, chunk, send, recv
        self.started = []

    def copy(self, way, step, dz):
        ref = self.buf.at[self.chunk, wrap(self.place.z + dz, Z)]
        if step == 3:
            ref = ref.at[pl.ds(way * HD, HD)]
        index = (self.chunk * 2 + way) * 4 + step
        return pltpu.make_async_remote_copy(
            src_ref=ref,
            dst_ref=ref,
            send_sem=self.send.at[index],
            recv_sem=self.recv.at[index],
            device_id=self.place.at_z(1 - 2 * way),
            device_id_type=MESH,
        )

    def go(self, step):
        for way in range(2):
            copy = self.copy(way, step, -step if way == 0 else step)
            copy.start()
            self.started.append(copy)

    def take(self, step):
        for way in range(2):
            self.copy(way, step, -1 - step if way == 0 else 1 + step).wait_recv()

    def finish(self):
        for copy in self.started:
            copy.wait_send()


def kernel(
    hidden_hbm, gain_ref, wq_hbm, enc_hbm, wk_hbm, wv_hbm, wo_hbm, count_ref, out_ref,
    hbuf, wq, wk, wv, wo, nbuf, ebuf, qbuf, kbuf, vbuf, sbuf, opart, spart,
    osend, orecv, ssend, srecv, attb,
    st1, rv1, st2, rv2, st3, rv3, st4, rv4, sums, msend, mrecv,
    local_sem, ms_ss, ms_rs, ag_ss, ag_rs, q_ss, q_rs, o_ss, o_rs, x_ss, x_rs,
):
    place = Place()
    me = place.head
    z = place.z

    local = [
        pltpu.make_async_copy(source, target, local_sem.at[index])
        for index, (source, target) in enumerate(
            (
                (hidden_hbm, hbuf),
                (enc_hbm, ebuf.at[me]),
                (wq_hbm, wq),
                (wk_hbm, wk),
                (wv_hbm, wv),
                (wo_hbm, wo),
            )
        )
    ]
    for copy in local:
        copy.start()

    barrier = pltpu.get_barrier_semaphore()
    partners = [place.at_xy(d, 0) for d in (1, 2, 3)]
    partners += [place.at_xy(0, d) for d in (1, 2, 3)]
    partners += [place.at_z(1), place.at_z(-1)]
    for partner in partners:
        pl.semaphore_signal(barrier, inc=1, device_id=partner, device_id_type=MESH)

    for chunk in range(CHUNKS):
        orecv[chunk, 0, 0, HD:] = jnp.zeros((HD, T), BF16)
        orecv[chunk, 1, 0, :HD] = jnp.zeros((HD, T), BF16)

    local[0].wait()
    hid = hbuf[...].astype(F32)
    squares = hid * hid
    squares = squares[:, :128] + squares[:, 128:]
    total = jnp.sum(squares.T, axis=0, keepdims=True)
    pl.semaphore_wait(barrier, len(partners))
    ms_started = []

    def ms_copy(stage, d):
        index = stage * 3 + d - 1
        to = place.at_xy(0, d) if stage == 0 else place.at_xy(d, 0)
        return pltpu.make_async_remote_copy(
            src_ref=msend.at[stage],
            dst_ref=mrecv.at[stage, d - 1],
            send_sem=ms_ss.at[index],
            recv_sem=ms_rs.at[index],
            device_id=to,
            device_id_type=MESH,
        )

    def ms_send(stage, value):
        msend[stage] = jnp.broadcast_to(value, (8, CHUNKS * T))
        for d in (1, 2, 3):
            copy = ms_copy(stage, d)
            copy.start()
            ms_started.append(copy)

    def ms_take(stage, value):
        for d in (1, 2, 3):
            ms_copy(stage, d).wait_recv()
        for d in (1, 2, 3):
            value = value + mrecv[stage, d - 1, 0:1, :]
        return value

    gather_e = Gather(place, ebuf, BLOCK, ag_ss.at[0], ag_rs.at[0])
    gather_a = Gather(place, nbuf.at[0], T, ag_ss.at[1], ag_rs.at[1])
    gather_b = Gather(place, nbuf.at[1], T, ag_ss.at[2], ag_rs.at[2])
    ring_a = QueryRing(place, qbuf, 0, q_ss, q_rs)
    ring_b = QueryRing(place, qbuf, 1, q_ss, q_rs)

    ms_send(0, total)
    local[1].wait()
    gather_e.s0()
    total = ms_take(0, total)
    ms_send(1, total)
    total = ms_take(1, total)
    inverse = lax.rsqrt(total * (1.0 / (HEAD * F)) + 1e-05)
    column = jnp.broadcast_to(inverse, (128, CHUNKS * T)).T
    gain = gain_ref[...].astype(F32)
    for side in range(2):
        cols = pl.ds(side * 128, 128)
        normed = hbuf[:, cols].astype(F32) * column * gain[:, side * 128 : side * 128 + 128]
        normed = normed.astype(BF16)
        for chunk in range(CHUNKS):
            nbuf[chunk, pl.ds(me, 1), :, cols] = normed[chunk * T : (chunk + 1) * T][None]

    def project(chunk):
        acc = jnp.zeros((T, F), F32)
        for source in range(HEAD):
            acc = acc + jnp.dot(
                nbuf[chunk, source], wq[source * F : (source + 1) * F], preferred_element_type=F32
            )
        qbuf[chunk, pl.ds(z, 1)] = acc.T.astype(BF16)[None]

    live_blocks = count_ref[z]

    def live_mask(block, shape):
        return (jnp.zeros(shape, jnp.int32) + block) < live_blocks

    def encode(part):
        rows = ebuf[4 * part : 4 * part + 4].reshape(4 * BLOCK, DE)
        keys = jnp.dot(rows, wk[...], preferred_element_type=F32)
        values = jnp.dot(rows, wv[...], preferred_element_type=F32)
        for inner in range(4):
            block = 4 * part + inner
            live = live_mask(block, (BLOCK, HD))
            span = slice(inner * BLOCK, (inner + 1) * BLOCK)
            for head in range(2):
                cols = slice(head * HD, (head + 1) * HD)
                key_block = keys[span, cols]
                if block > 0:
                    key_block = jnp.where(live, key_block, kbuf[head, :BLOCK].astype(F32))
                kbuf[head, block * BLOCK : (block + 1) * BLOCK] = key_block.astype(BF16)
                value_block = jnp.where(live, values[span, cols], 0.0)
                vbuf[cols, block * BLOCK : (block + 1) * BLOCK] = value_block.T.astype(BF16)

    gather_a.s0()
    gather_b.s0()
    gather_a.s1()
    gather_a.s2()
    gather_a.s3()
    gather_b.s1()
    gather_a.s4()
    gather_a.s5()
    gather_b.s2()
    gather_b.s3()
    gather_a.s6()
    local[2].wait()
    project(0)
    ring_a.go(0)
    gather_b.s4()
    gather_b.s5()
    gather_e.s1()
    ring_a.take(0)
    ring_a.go(1)
    gather_e.s2()
    gather_e.s3()
    gather_b.s6()
    project(1)
    ring_b.go(0)
    ring_a.take(1)
    ring_a.go(2)
    gather_e.s4()
    ring_a.take(2)
    ring_a.go(3)
    ring_b.take(0)
    ring_b.go(1)
    gather_e.s5()
    ring_b.take(1)
    ring_b.go(2)
    gather_e.s6()
    ring_b.take(2)
    ring_b.go(3)
    local[3].wait()
    local[4].wait()
    for part in range(4):
        encode(part)
    ring_a.take(3)
    ring_b.take(3)
    local[5].wait()

    live_row = [jnp.where(live_mask(block, (1, T)), 1.0, 0.0) for block in range(SLOTS)]

    def attend(chunk, plane):
        for head in range(2):
            query = qbuf[chunk, pl.ds(plane, 1), head * HD : (head + 1) * HD, :][0]
            best = None
            for piece in range(KEYS // 256):
                span = slice(piece * 256, (piece + 1) * 256)
                scores = jnp.dot(kbuf[head, span], query, preferred_element_type=F32)
                sbuf[head, span] = scores
                top = jnp.max(scores.reshape(32, 8, T), axis=0)
                best = top if best is None else jnp.maximum(best, top)
            best = jnp.max(best, axis=0, keepdims=True) * COEF
            acc = jnp.zeros((HD, T), F32)
            total = jnp.zeros((8, T), F32)
            for piece in range(KEYS // 256):
                span = slice(piece * 256, (piece + 1) * 256)
                weights = jnp.exp2(sbuf[head, span] * COEF - best)
                for inner in range(2):
                    block_sum = jnp.sum(
                        weights[inner * BLOCK : (inner + 1) * BLOCK].reshape(16, 8, T), axis=0
                    )
                    total = total + block_sum * live_row[piece * 2 + inner]
                acc = acc + jnp.dot(
                    vbuf[head * HD : (head + 1) * HD, span],
                    weights.astype(BF16),
                    preferred_element_type=F32,
                )
            opart[head * HD : (head + 1) * HD] = acc
            spart[2 * head : 2 * head + 1] = best
            spart[2 * head + 1 : 2 * head + 2] = jnp.sum(total, axis=0, keepdims=True)

    def merge(chunk, way, step):
        for head in range(2):
            rows = slice(head * HD, (head + 1) * HD)
            best_a = spart[2 * head : 2 * head + 1]
            best_b = srecv[chunk, way, step, 2 * head : 2 * head + 1, :]
            sum_a = spart[2 * head + 1 : 2 * head + 2]
            sum_b = srecv[chunk, way, step, 2 * head + 1 : 2 * head + 2, :]
            best = jnp.maximum(best_a, best_b)
            scale_a = jnp.exp2(best_a - best)
            scale_b = jnp.exp2(best_b - best)
            spart[2 * head : 2 * head + 1] = best
            spart[2 * head + 1 : 2 * head + 2] = sum_a * scale_a + sum_b * scale_b
            opart[rows] = (
                opart[rows] * scale_a + orecv[chunk, way, step, rows, :].astype(F32) * scale_b
            )

    def o_copies(chunk, way, step, first):
        index = ((chunk * 2 + way) * 4 + step) * 2
        to = (place.dp, wrap(z + 1 - 2 * way, Z), place.head)
        source, target = osend.at[chunk, way, step], orecv.at[chunk, way, step]
        if first:
            source, target = source.at[pl.ds(way * HD, HD)], target.at[pl.ds(way * HD, HD)]
        return [
            pltpu.make_async_remote_copy(
                src_ref=src,
                dst_ref=dst,
                send_sem=o_ss.at[index + which],
                recv_sem=o_rs.at[index + which],
                device_id=to,
                device_id_type=MESH,
            )
            for which, (src, dst) in enumerate(
                ((source, target), (ssend.at[chunk, way, step], srecv.at[chunk, way, step]))
            )
        ]

    def out_axes(half, da, db):
        return (da, db) if half == 0 else (db, da)

    def out_copy(chunk, half, way, step):
        send, recv = ((st1, rv1), (st2, rv2), (st3, rv3), (st4, rv4))[step]
        off = 1 - 2 * way
        to = place.at_xy(*out_axes(half, off, 0) if step < 2 else out_axes(half, 0, off))
        index = ((chunk * 2 + half) * 2 + way) * 4 + step
        return pltpu.make_async_remote_copy(
            src_ref=send.at[chunk, half, way],
            dst_ref=recv.at[chunk, half, way],
            send_sem=x_ss.at[index],
            recv_sem=x_rs.at[index],
            device_id=to,
            device_id_type=MESH,
        )

    def out_part(chunk, half, da, db):
        slot = place.slot(*out_axes(half, da, db))
        return jnp.dot(
            attb[chunk, half * 128 : (half + 1) * 128],
            wo[:, pl.ds(pl.multiple_of(slot * F, F), F)],
            preferred_element_type=F32,
        )

    def out_take(chunk, step):
        for half in range(2):
            for way in range(2):
                out_copy(chunk, half, way, step).wait_recv()

    def out_1(chunk):
        for half in range(2):
            for db in range(4):
                part = out_part(chunk, half, 2, db).astype(BF16)
                st1[chunk, half, 0, db] = part[:64]
                st1[chunk, half, 1, db] = part[64:]
            for way in range(2):
                out_copy(chunk, half, way, 0).start()

    def out_2(chunk):
        out_take(chunk, 0)
        for half in range(2):
            for way in range(2):
                for db in range(4):
                    part = out_part(chunk, half, 1 - 2 * way, db)
                    other = rv1[chunk, half, way, db].astype(F32)
                    if way == 0:
                        st2[chunk, half, way, db, :64] = (part[:64] + other).astype(BF16)
                        st2[chunk, half, way, db, 64:] = part[64:].astype(BF16)
                    else:
                        st2[chunk, half, way, db, :64] = part[:64].astype(BF16)
                        st2[chunk, half, way, db, 64:] = (part[64:] + other).astype(BF16)
                out_copy(chunk, half, way, 1).start()

    def out_3(chunk):
        out_take(chunk, 1)
        for half in range(2):
            for db in (2, 1, 3, 0):
                part = out_part(chunk, half, 0, db)
                part = part + rv2[chunk, half, 0, db].astype(F32)
                part = part + rv2[chunk, half, 1, db].astype(F32)
                if db == 2:
                    st3[chunk, half, 0] = part[:64].astype(BF16)
                    st3[chunk, half, 1] = part[64:].astype(BF16)
                    for way in range(2):
                        out_copy(chunk, half, way, 2).start()
                else:
                    sums[half, (1, 3, 0).index(db)] = part

    def out_4(chunk):
        out_take(chunk, 2)
        for half in range(2):
            part = sums[half, 0]
            st4[chunk, half, 0, :64] = (part[:64] + rv3[chunk, half, 0].astype(F32)).astype(BF16)
            st4[chunk, half, 0, 64:] = part[64:].astype(BF16)
            out_copy(chunk, half, 0, 3).start()
            part = sums[half, 1]
            st4[chunk, half, 1, :64] = part[:64].astype(BF16)
            st4[chunk, half, 1, 64:] = (part[64:] + rv3[chunk, half, 1].astype(F32)).astype(BF16)
            out_copy(chunk, half, 1, 3).start()

    def out_5(chunk):
        out_take(chunk, 3)
        for half in range(2):
            part = sums[half, 2] + rv4[chunk, half, 0].astype(F32)
            part = part + rv4[chunk, half, 1].astype(F32)
            start = chunk * T + half * 128
            out_ref[start : start + 128] = part.astype(BF16)

    def one_block(n, carry):
        chunk = lax.div(n, 8)
        i = lax.rem(n, 8)
        step = lax.div(i + 1, 2)
        way = lax.rem(i + 1, 2)
        plane = wrap(z + (1 - 2 * way) * (4 - step), Z)
        attend(chunk, plane)

        @pl.when(i == 0)
        def _():
            neutral_best = jnp.full((1, T), NEG, F32)
            neutral_sum = jnp.zeros((1, T), F32)
            for w in range(2):
                rows = slice(w * HD, (w + 1) * HD)
                osend[chunk, w, 0, rows] = opart[rows].astype(BF16)
                ssend[chunk, w, 0, 2 * w : 2 * w + 2] = spart[2 * w : 2 * w + 2]
                o = 1 - w
                ssend[chunk, w, 0, 2 * o : 2 * o + 1] = neutral_best
                ssend[chunk, w, 0, 2 * o + 1 : 2 * o + 2] = neutral_sum
                for copy in o_copies(chunk, w, 0, True):
                    copy.start()

        @pl.when(jnp.logical_and(i > 0, i < 7))
        def _():
            @pl.when(step == 1)
            def _():
                first_take(chunk, way)

            @pl.when(step > 1)
            def _():
                for copy in o_copies(chunk, way, step - 1, False):
                    copy.wait_recv()

            merge(chunk, way, step - 1)
            osend[chunk, way, step] = opart[...].astype(BF16)
            ssend[chunk, way, step] = spart[...]
            for copy in o_copies(chunk, way, step, False):
                copy.start()

        @pl.when(i == 7)
        def _():
            for w in range(2):
                for copy in o_copies(chunk, w, 3, False):
                    copy.wait_recv()
                merge(chunk, w, 3)
            for head in range(2):
                rows = slice(head * HD, (head + 1) * HD)
                done = opart[rows] / spart[2 * head + 1 : 2 * head + 2]
                attb[chunk, :, rows] = done.T.astype(BF16)

        for at, work in ((8, out_1), (10, out_2), (12, out_3), (14, out_4)):
            pl.when(n == at)(lambda work=work: work(0))
        return carry

    def first_take(chunk, way):
        for w in range(2):
            @pl.when(way == w)
            def _():
                for copy in o_copies(chunk, w, 0, True):
                    copy.wait_recv()

    spart[...] = jnp.zeros((8, T), F32)
    lax.fori_loop(0, 8 * CHUNKS, one_block, 0)
    out_5(0)
    out_1(1)
    out_2(1)
    out_3(1)
    out_4(1)
    out_5(1)

    for copy in ms_started:
        copy.wait_send()
    for gather in (gather_e, gather_a, gather_b, ring_a, ring_b):
        gather.finish()
    for chunk in range(CHUNKS):
        for way in range(2):
            for step in range(4):
                for copy in o_copies(chunk, way, step, step == 0):
                    copy.wait_send()
                for half in range(2):
                    out_copy(chunk, half, way, step).wait_send()


def per_device(hidden_in, norm_gain, w_query, enc_states, w_key, w_value, w_out, block_counts):
    any_spec = pl.BlockSpec(memory_space=pl.ANY)
    vmem = pltpu.VMEM
    dma = pltpu.SemaphoreType.DMA
    scratch = [
        vmem((CHUNKS * T, F), BF16),
        vmem((HEAD * F, F), BF16),
        vmem((DE, F), BF16),
        vmem((DE, F), BF16),
        vmem((F, HEAD * F), BF16),
        vmem((CHUNKS, HEAD, T, F), BF16),
        vmem((HEAD, BLOCK, DE), BF16),
        vmem((CHUNKS, Z, F, T), BF16),
        vmem((2, KEYS, HD), BF16),
        vmem((F, KEYS), BF16),
        vmem((2, KEYS, T), F32),
        vmem((F, T), F32),
        vmem((8, T), F32),
        vmem((CHUNKS, 2, 4, F, T), BF16),
        vmem((CHUNKS, 2, 4, F, T), BF16),
        vmem((CHUNKS, 2, 4, 8, T), F32),
        vmem((CHUNKS, 2, 4, 8, T), F32),
        vmem((CHUNKS, T, F), BF16),
        vmem((CHUNKS, 2, 2, 4, 64, F), BF16),
        vmem((CHUNKS, 2, 2, 4, 64, F), BF16),
        vmem((CHUNKS, 2, 2, 4, 128, F), BF16),
        vmem((CHUNKS, 2, 2, 4, 128, F), BF16),
        vmem((CHUNKS, 2, 2, 64, F), BF16),
        vmem((CHUNKS, 2, 2, 64, F), BF16),
        vmem((CHUNKS, 2, 2, 128, F), BF16),
        vmem((CHUNKS, 2, 2, 128, F), BF16),
        vmem((2, 3, 128, F), F32),
        vmem((2, 8, CHUNKS * T), F32),
        vmem((2, 3, 8, CHUNKS * T), F32),
        dma((6,)),
        dma((6,)),
        dma((6,)),
        dma((3, 40)),
        dma((3, 40)),
        dma((CHUNKS * 8,)),
        dma((CHUNKS * 8,)),
        dma((CHUNKS * 16,)),
        dma((CHUNKS * 16,)),
        dma((CHUNKS * 16,)),
        dma((CHUNKS * 16,)),
    ]
    return pl.pallas_call(
        kernel,
        out_shape=jax.ShapeDtypeStruct((CHUNKS * T, F), BF16),
        in_specs=[
            any_spec,
            pl.BlockSpec(memory_space=pltpu.VMEM),
            any_spec,
            any_spec,
            any_spec,
            any_spec,
            any_spec,
            pl.BlockSpec(memory_space=pltpu.SMEM),
        ],
        out_specs=pl.BlockSpec(memory_space=pltpu.VMEM),
        scratch_shapes=scratch,
        compiler_params=pltpu.CompilerParams(
            collective_id=0, has_side_effects=True, vmem_limit_bytes=60 * 1024 * 1024
        ),
        cost_estimate=pl.CostEstimate(
            flops=13_000_000_000, bytes_accessed=8_000_000, transcendentals=17_000_000
        ),
    )(
        hidden_in, norm_gain.reshape(1, F), w_query, enc_states, w_key, w_value, w_out, block_counts
    )


def solution(mesh):
    placed = (
        P(("dp", "span"), "head"),
        P("head"),
        P(None, "head"),
        P(("dp", "span", "head"), None),
        P(None, "head"),
        P(None, "head"),
        P("head", None),
        P("dp"),
    )
    return jax.shard_map(
        per_device, mesh=mesh, in_specs=placed, out_specs=P(("dp", "span"), "head"), check_vma=False
    )
```

time: 528 us -> 145 us (0.27)
  waiting for transfers between devices: 347 us -> 0 us
  Pallas kernels: 0 us -> 142 us
  local copies, waits for them, and re-layouts: 71.6 us -> 2.89 us
  matrix products: 48.6 us -> 0 us
  other arithmetic: 21.5 us -> 0 us
  blocking collectives: 21.1 us -> 0 us
  between operations: 13.2 us -> 0.01 us
    all_gather x3 -> x0, waiting for transfers between devices: 265 us -> none  [the longest x1 168 us: per_device(): portion = lax.all_gather(group_kv, 'span', axis=1, tiled=True)]
    pallas_call x0 -> x1, Pallas kernels: none -> 142 us  [per_device(): pl.pallas_call(kernel, out_shape=jax.ShapeDtypeStruct((CHUNKS * T, F), BF...]
    reduce_scatter x1 -> x0, waiting for transfers between devices: 81.2 us -> none  [per_device(): lax.psum_scatter(partial_out.astype(jnp.bfloat16), 'head', scatter_dimens...]
    dot_general x68 -> x0, matrix products: 48.6 us -> none  [the longest x32 19.4 us: tile_work(): jnp.einsum('hqk,khd->qhd', weights.astype(jnp.bfloat16), value_heads, pre...]
    while x224 -> x0, local copies, waits for them, and re-layouts: 34.2 us -> none
    slice x32 -> x0, local copies, waits for them, and re-layouts: 34 us -> none  [tile_work(): value_heads = key_block[1].reshape(tile_rows, heads_local, HD)]
    all_gather x1 -> x0, blocking collectives: 21.1 us -> none  [per_device(): lax.all_gather(norm_gain, 'head', axis=0, tiled=True)]
    reduce_sum x34 -> x0, other arithmetic: 17.8 us -> none  [the longest x32 14.3 us: tile_work(): running_sum = running_sum * factor + jnp.sum(weights, axis=2)]
  transfers between devices with their start and end apart: 4 -> 0, of which waited for: 4 -> 0; matrix products, arithmetic and copies ran while one was open for 3% -> 0% of each run, Pallas kernels for 0% -> 0%
where the time goes in v1:
time: 145 us
  Pallas kernels  142 us (98%)
  local copies, waits for them, and re-layouts  2.89 us (2%)
    pallas_call x1, Pallas kernels, per_device(): pl.pallas_call(kernel, out_shape=jax.ShapeDtypeStruct((CHUNKS * T, F), BF...  142 us

profile of v1, /device:TPU:2, one launch (start us, length us, event | category | flops | bytes accessed | tf_op | source)
XLA Modules:
  0.0 145.2 jit_solution(5253765874895287897)
XLA Ops:
  0.0 1.2 reshape.3.gain_ref
  1.2 142.3 %shard_map.82 = bf16[512,256]{1,0:T(8,128)(2,1)} custom-call(bf16[512,256]{1,0:T(8,128)(2,1)} %hidden_hbm.1, bf16[1,256]{1,0:T(2,128)(2,1)} %reshape.3.gain_ref, bf16[4096,256]{1,0:T(8,128)(2,1)} %wq_hbm.1, bf16[128,1024]{1,0:T(8,128)(2,1)} %enc_hbm.1, bf16[1024,256]{1,0:T(8,128)(2,1)} %wk_hbm.1, bf16[1024,256]{1,0:T(8,128)(2,1)} %wv_hbm.1, ...), custom_call_target="tpu_custom_call" | custom-call | flops 12999999488 | bytes 8000000 | tf_op jit(solution)/shard_map/pallas_call | solution.py:646
  143.5 1.7 %copy.10 = bf16[512,256]{1,0:T(8,128)(2,1)} copy(bf16[512,256]{1,0:T(8,128)(2,1)} %shard_map.82) | data formatting | bytes 524288

commit v2 on v1

v2 whole, which is shorter than its diff:
```python
import math

import jax
import jax.numpy as jnp
from jax import lax
from jax.experimental import pallas as pl
from jax.experimental.pallas import tpu as pltpu
from jax.sharding import PartitionSpec as P

HD = 128
X = 4
Y = 4
Z = 8
HEAD = X * Y
T = 256
CHUNKS = 2
F = 256
BLOCK = 128
SLOTS = 16
KEYS = BLOCK * SLOTS
TILE = 256
DE = 1024
LOG2E = 1.4426950408889634
COEF = LOG2E / math.sqrt(HD)
NEG = -1e30
F32 = jnp.float32
BF16 = jnp.bfloat16
MESH = pl.DeviceIdType.MESH


def div(value, by):
    return value // by if isinstance(value, int) else lax.div(value, by)


def rem(value, by):
    return value % by if isinstance(value, int) else lax.rem(value, by)


def wrap(value, size):
    return rem(value + 2 * size, size)


class Place:
    def __init__(self):
        self.dp = lax.axis_index("dp")
        self.z = lax.axis_index("span")
        self.head = lax.axis_index("head")
        self.x = div(self.head, Y)
        self.y = rem(self.head, Y)

    def slot(self, dx, dy):
        return wrap(self.x + dx, X) * Y + wrap(self.y + dy, Y)

    def at_xy(self, dx, dy):
        return (self.dp, self.z, self.slot(dx, dy))

    def at_z(self, dz):
        return (self.dp, wrap(self.z + dz, Z), self.head)


class Gather:
    REL = (0, -1, 1, 2)

    def __init__(self, place, buf, rows, send, recv):
        self.place, self.buf, self.rows, self.send, self.recv = place, buf, rows, send, recv
        self.started = []

    def shift(self, half, da, db):
        return (db, da) if half == 0 else (da, db)

    def part(self, half, da, db, quarter):
        base = half * (self.rows // 2)
        count = self.rows // 2
        if quarter is not None:
            count = self.rows // 4
            base = base + quarter * count
        return self.buf.at[self.place.slot(*self.shift(half, da, db)), pl.ds(base, count)]

    def copy(self, half, index, ref, to):
        return pltpu.make_async_remote_copy(
            src_ref=ref,
            dst_ref=ref,
            send_sem=self.send.at[half * 20 + index],
            recv_sem=self.recv.at[half * 20 + index],
            device_id=to,
            device_id_type=MESH,
        )

    def sent(self, half, index, da, db, quarter, ta, tb):
        ref = self.part(half, da, db, quarter)
        return self.copy(half, index, ref, self.place.at_xy(*self.shift(half, ta, tb)))

    def go(self, *what):
        self.sent(*what).start()
        self.started.append(what)

    def take(self, half, index, da, db, quarter):
        ref = self.part(half, da, db, quarter)
        self.copy(half, index, ref, self.place.at_xy(1, 0)).wait_recv()

    def line(self, half, which):
        base = 4 + 4 * which
        rel = self.REL[which]
        self.go(half, base, rel, 0, None, 0, 1)
        self.go(half, base + 1, rel, 0, None, 0, -1)

    def pass_on(self, half, which):
        base = 4 + 4 * which
        rel = self.REL[which]
        self.take(half, base, rel, -1, None)
        self.go(half, base + 2, rel, -1, 0, 0, 1)
        self.take(half, base + 1, rel, 1, None)
        self.go(half, base + 3, rel, 1, 1, 0, -1)

    def s0(self):
        for half in range(2):
            self.go(half, 0, 0, 0, None, 1, 0)
            self.go(half, 1, 0, 0, None, -1, 0)
        for half in range(2):
            self.line(half, 0)

    def s1(self):
        for half in range(2):
            self.take(half, 0, -1, 0, None)
            self.go(half, 2, -1, 0, 0, 1, 0)
            self.take(half, 1, 1, 0, None)
            self.go(half, 3, 1, 0, 1, -1, 0)
        for half in range(2):
            self.line(half, 1)
            self.line(half, 2)

    def s2(self):
        for half in range(2):
            self.pass_on(half, 0)

    def s3(self):
        for half in range(2):
            self.take(half, 2, 2, 0, 0)
            self.take(half, 3, 2, 0, 1)
            self.line(half, 3)

    def s4(self):
        for which in (1, 2):
            for half in range(2):
                self.pass_on(half, which)

    def s5(self):
        for half in range(2):
            self.pass_on(half, 3)

    def s6(self):
        for which in range(4):
            for half in range(2):
                base = 4 + 4 * which
                rel = self.REL[which]
                self.take(half, base + 2, rel, 2, 0)
                self.take(half, base + 3, rel, 2, 1)

    def finish(self):
        for what in self.started:
            self.sent(*what).wait_send()


class QueryRing:
    def __init__(self, place, buf, chunk, send, recv):
        self.place, self.buf, self.chunk, self.send, self.recv = place, buf, chunk, send, recv
        self.started = []

    def copy(self, way, step, head, dz):
        ref = self.buf.at[self.chunk, wrap(self.place.z + dz, Z), pl.ds(head * HD, HD)]
        index = ((self.chunk * 2 + way) * 4 + step) * 2 + head
        return pltpu.make_async_remote_copy(
            src_ref=ref,
            dst_ref=ref,
            send_sem=self.send.at[index],
            recv_sem=self.recv.at[index],
            device_id=self.place.at_z(1 - 2 * way),
            device_id_type=MESH,
        )

    def go(self, way, step, head):
        if step == 3 and head != way:
            return
        what = (way, step, head, -step if way == 0 else step)
        self.copy(*what).start()
        self.started.append(what)

    def begin(self):
        for head in range(2):
            for way in range(2):
                self.go(way, 0, head)

    def hop(self, step):
        for head in range(2):
            for way in range(2):
                if step == 3 and head != way:
                    continue
                self.copy(way, step, head, -1 - step if way == 0 else 1 + step).wait_recv()
                if step < 3:
                    self.go(way, step + 1, head)

    def finish(self):
        for what in self.started:
            self.copy(*what).wait_send()


def kernel(
    hidden_hbm, gain_ref, wq_hbm, enc_hbm, wk_hbm, wv_hbm, wo_hbm, count_ref, out_ref,
    wq, wk, wv, wo, nbuf, ebuf, qbuf, kbuf, vbuf, score_0, score_1, best_0, best_1, blocks_o, blocks_s, live_buf,

    osend, orecv, attb,
    st1, rv1, st2, rv2, st3, rv3, st4, rv4, parts, gains,
    local_sem, ms_ss, ms_rs, ag_ss, ag_rs, q_ss, q_rs, o_ss, o_rs, x_ss, x_rs,
):
    place = Place()
    me = place.head
    z = place.z

    local = [
        pltpu.make_async_copy(source, target, local_sem.at[index])
        for index, (source, target) in enumerate(
            (
                (hidden_hbm.at[pl.ds(0, T)], nbuf.at[0, me]),
                (hidden_hbm.at[pl.ds(T, T)], nbuf.at[1, me]),
                (enc_hbm, ebuf.at[me]),
                (wq_hbm, wq),
                (wk_hbm, wk),
                (wv_hbm, wv),
                (wo_hbm, wo),
            )
        )
    ]
    for copy in local:
        copy.start()

    barrier = pltpu.get_barrier_semaphore()
    partners = [place.at_xy(d, 0) for d in (1, 2, 3)]
    partners += [place.at_xy(0, d) for d in (1, 2, 3)]
    partners += [place.at_z(1), place.at_z(-1)]
    for partner in partners:
        pl.semaphore_signal(barrier, inc=1, device_id=partner, device_id_type=MESH)

    gains[pl.ds(me, 1)] = jnp.broadcast_to(gain_ref[...].astype(F32).reshape(1, 1, F), (1, 8, F))

    def gain_copy(stage, d, behind=0):
        if stage == 0:
            ref, to = gains.at[place.slot(0, -behind)], place.at_xy(0, d)
        else:
            ref, to = gains.at[pl.ds(wrap(place.x - behind, X) * Y, Y)], place.at_xy(d, 0)
        return pltpu.make_async_remote_copy(
            src_ref=ref,
            dst_ref=ref,
            send_sem=ms_ss.at[stage * 3 + d - 1],
            recv_sem=ms_rs.at[stage * 3 + d - 1],
            device_id=to,
            device_id_type=MESH,
        )

    def gain_go(stage):
        for d in (1, 2, 3):
            gain_copy(stage, d).start()

    def gain_take(stage):
        for d in (1, 2, 3):
            gain_copy(stage, d, d).wait_recv()

    gather_e = Gather(place, ebuf, BLOCK, ag_ss.at[0], ag_rs.at[0])
    gather_a = Gather(place, nbuf.at[0], T, ag_ss.at[1], ag_rs.at[1])
    gather_b = Gather(place, nbuf.at[1], T, ag_ss.at[2], ag_rs.at[2])
    ring_a = QueryRing(place, qbuf, 0, q_ss, q_rs)
    ring_b = QueryRing(place, qbuf, 1, q_ss, q_rs)

    def project(chunk):
        squares = jnp.zeros((T, F), F32)
        for source in range(HEAD):
            rows = nbuf[chunk, source].astype(F32)
            squares = squares + rows * rows
        mean = jnp.sum(squares, axis=1, keepdims=True) * (1.0 / (HEAD * F))
        inverse = lax.rsqrt(mean + 1e-05)
        acc = jnp.zeros((T, F), F32)
        for source in range(HEAD):
            rows = nbuf[chunk, source].astype(F32) * inverse * gains[source, 0:1, :]
            acc = acc + jnp.dot(
                rows.astype(BF16), wq[source * F : (source + 1) * F], preferred_element_type=F32
            )
        qbuf[chunk, pl.ds(z, 1)] = acc.T.astype(BF16)[None]

    live_blocks = count_ref[z]

    def encode():
        for part in range(4):
            rows = ebuf[4 * part : 4 * part + 4].reshape(4 * BLOCK, DE)
            keys = jnp.dot(rows, wk[...], preferred_element_type=F32)
            values = jnp.dot(rows, wv[...], preferred_element_type=F32)
            slot = lax.broadcasted_iota(jnp.int32, (4 * BLOCK, HD), 0) // BLOCK + 4 * part
            live = slot < live_blocks
            span = pl.ds(part * 4 * BLOCK, 4 * BLOCK)
            for head in range(2):
                cols = slice(head * HD, (head + 1) * HD)
                key_block = keys[:, cols]
                lead = key_block[:BLOCK] if part == 0 else kbuf[head, :BLOCK].astype(F32)
                lead = jnp.concatenate([lead] * 4, axis=0)
                kbuf[head, span] = jnp.where(live, key_block, lead).astype(BF16)
                vbuf[cols, span] = jnp.where(live, values[:, cols], 0.0).T.astype(BF16)

    blocks_s[...] = jnp.zeros((CHUNKS * Z, 8, T), F32)
    for slot in range(SLOTS):
        alive = (jnp.zeros((8, T), jnp.int32) + slot) < live_blocks
        live_buf[slot] = jnp.where(alive, 1.0, 0.0)

    pl.semaphore_wait(barrier, len(partners))
    local[0].wait()
    gather_a.s0()
    local[1].wait()
    gather_b.s0()
    gain_go(0)
    gather_a.s1()
    gather_a.s2()
    gain_take(0)
    gain_go(1)
    gather_a.s3()
    gather_b.s1()
    gather_a.s4()
    gather_a.s5()
    gather_b.s2()
    gather_b.s3()
    gather_a.s6()
    gain_take(1)
    local[3].wait()
    project(0)
    ring_a.begin()
    gather_b.s4()
    gather_b.s5()
    local[2].wait()
    gather_e.s0()
    ring_a.hop(0)
    gather_b.s6()
    project(1)
    ring_b.begin()
    ring_a.hop(1)
    gather_e.s1()
    ring_b.hop(0)
    gather_e.s2()
    gather_e.s3()
    ring_a.hop(2)
    ring_b.hop(1)
    gather_e.s4()
    ring_a.hop(3)
    ring_b.hop(2)
    gather_e.s5()
    ring_b.hop(3)
    gather_e.s6()
    local[4].wait()
    local[5].wait()
    encode()
    local[6].wait()

    score_buf = (score_0, score_1)
    best_buf = (best_0, best_1)

    def sides(i):
        step = div(i + 1, 2)
        way = rem(i + 1, 2)
        return step, way, wrap(z + (1 - 2 * way) * (4 - step), Z)

    def phase(soft, soft_head, block, head):
        if block is not None:
            query = qbuf[div(block, 8), sides(rem(block, 8))[2], pl.ds(head * HD, HD), :]
            top = None
        if soft is not None:
            best = best_buf[soft_head][0:1, :]
            acc = jnp.zeros((HD, T), F32)
            total = jnp.zeros((8, T), F32)
        for tile in range(KEYS // TILE):
            span = slice(tile * TILE, (tile + 1) * TILE)
            if block is not None:
                scores = jnp.dot(kbuf[head, span], query, preferred_element_type=F32)
                score_buf[head][span] = scores
                peak = jnp.max(scores.reshape(TILE // 8, 8, T), axis=0)
                top = peak if top is None else jnp.maximum(top, peak)
            if soft is not None:
                weights = jnp.exp2(score_buf[soft_head][span] * COEF - best)
                for inner in range(TILE // BLOCK):
                    rows = weights[inner * BLOCK : (inner + 1) * BLOCK]
                    rows = jnp.sum(rows.reshape(BLOCK // 8, 8, T), axis=0)
                    total = total + rows * live_buf[tile * (TILE // BLOCK) + inner]
                acc = acc + jnp.dot(
                    vbuf[soft_head * HD : (soft_head + 1) * HD, span],
                    weights.astype(BF16),
                    preferred_element_type=F32,
                )
        if block is not None:
            top = jnp.max(top, axis=0, keepdims=True) * COEF
            best_buf[head][...] = jnp.broadcast_to(top, (8, T))
        if soft is not None:
            blocks_o[soft, pl.ds(soft_head * HD, HD)] = acc
            blocks_s[soft, pl.ds(2 * soft_head, 1)] = best
            blocks_s[soft, pl.ds(2 * soft_head + 1, 1)] = jnp.sum(total, axis=0, keepdims=True)

    def split3(value):
        high = value.astype(BF16).astype(F32)
        middle = (value - high).astype(BF16).astype(F32)
        return [high, middle, value - high - middle]

    def o_copy(chunk, way, step, head):
        index = ((chunk * 2 + way) * 4 + step) * 2 + head
        return pltpu.make_async_remote_copy(
            src_ref=osend.at[chunk, way, step, head],
            dst_ref=orecv.at[chunk, way, step, head],
            send_sem=o_ss.at[index],
            recv_sem=o_rs.at[index],
            device_id=(place.dp, wrap(z + 1 - 2 * way, Z), place.head),
            device_id_type=MESH,
        )

    def send_part(chunk, block, way, step, head):
        osend[chunk, way, step, head, :HD] = blocks_o[block, pl.ds(head * HD, HD), :].astype(BF16)
        rows = split3(blocks_s[block, pl.ds(2 * head, 1), :])
        rows += split3(blocks_s[block, pl.ds(2 * head + 1, 1), :])
        rows = jnp.concatenate(rows + [jnp.zeros((10, T), F32)], axis=0)
        osend[chunk, way, step, head, HD:] = rows.astype(BF16)
        o_copy(chunk, way, step, head).start()

    def merge_part(chunk, block, way, step, head):
        o_copy(chunk, way, step, head).wait_recv()
        rows = pl.ds(head * HD, HD)
        best_row = pl.ds(2 * head, 1)
        sum_row = pl.ds(2 * head + 1, 1)
        stats = orecv[chunk, way, step, head, HD:, :].astype(F32)
        best_a = blocks_s[block, best_row, :]
        best_b = stats[0:1] + stats[1:2] + stats[2:3]
        sum_b = stats[3:4] + stats[4:5] + stats[5:6]
        best = jnp.maximum(best_a, best_b)
        scale_a = jnp.exp2(best_a - best)
        scale_b = jnp.exp2(best_b - best)
        blocks_s[block, best_row] = best
        blocks_s[block, sum_row] = blocks_s[block, sum_row, :] * scale_a + sum_b * scale_b
        blocks_o[block, rows] = (
            blocks_o[block, rows, :] * scale_a
            + orecv[chunk, way, step, head, :HD, :].astype(F32) * scale_b
        )

    def out_axes(half, da, db):
        return (da, db) if half == 0 else (db, da)

    def out_copy(chunk, half, way, step, db=0):
        send, recv = ((st1, rv1), (st2, rv2), (st3, rv3), (st4, rv4))[step]
        off = 1 - 2 * way
        to = place.at_xy(*out_axes(half, off, 0) if step < 2 else out_axes(half, 0, off))
        index = ((chunk * 2 + half) * 2 + way) * 10 + (step * 4 + db if step < 2 else 6 + step)
        source, target = send.at[chunk, half, way], recv.at[chunk, half, way]
        if step < 2:
            source, target = source.at[db], target.at[db]
        return pltpu.make_async_remote_copy(
            src_ref=source,
            dst_ref=target,
            send_sem=x_ss.at[index],
            recv_sem=x_rs.at[index],
            device_id=to,
            device_id_type=MESH,
        )

    def out_part(chunk, half, da, db):
        slot = place.slot(*out_axes(half, da, db))
        return jnp.dot(
            attb[chunk, half * 128 : (half + 1) * 128],
            wo[:, pl.ds(pl.multiple_of(slot * F, F), F)],
            preferred_element_type=F32,
        )

    ORDER = (2, 1, 3, 0)

    def out_1(chunk):
        for db in ORDER:
            for half in range(2):
                part = out_part(chunk, half, 2, db).astype(BF16)
                for way in range(2):
                    st1[chunk, half, way, db] = part[64 * way : 64 * way + 64]
                    out_copy(chunk, half, way, 0, db).start()
        for da in (1, 3, 0):
            for db in ORDER:
                for half in range(2):
                    parts[chunk, half, da, db] = out_part(chunk, half, da, db)

    def out_2(chunk):
        for db in ORDER:
            for half in range(2):
                for way in range(2):
                    same = slice(64 * way, 64 * way + 64)
                    rest = slice(64 - 64 * way, 128 - 64 * way)
                    da = (1, 3)[way]
                    st2[chunk, half, way, db, rest] = parts[chunk, half, da, db, rest].astype(BF16)
                    out_copy(chunk, half, way, 0, db).wait_recv()
                    part = parts[chunk, half, da, db, same] + rv1[chunk, half, way, db].astype(F32)
                    st2[chunk, half, way, db, same] = part.astype(BF16)
                    out_copy(chunk, half, way, 1, db).start()

    def out_3(chunk):
        for db in ORDER:
            for half in range(2):
                part = parts[chunk, half, 0, db]
                for way in range(2):
                    out_copy(chunk, half, way, 1, db).wait_recv()
                    part = part + rv2[chunk, half, way, db].astype(F32)
                if db == 2:
                    for way in range(2):
                        st3[chunk, half, way] = part[64 * way : 64 * way + 64].astype(BF16)
                        out_copy(chunk, half, way, 2).start()
                else:
                    parts[chunk, half, 0, db] = part

    def out_4(chunk):
        for half in range(2):
            for way in range(2):
                same = slice(64 * way, 64 * way + 64)
                rest = slice(64 - 64 * way, 128 - 64 * way)
                db = (1, 3)[way]
                st4[chunk, half, way, rest] = parts[chunk, half, 0, db, rest].astype(BF16)
                out_copy(chunk, half, way, 2).wait_recv()
                part = parts[chunk, half, 0, db, same] + rv3[chunk, half, way].astype(F32)
                st4[chunk, half, way, same] = part.astype(BF16)
                out_copy(chunk, half, way, 3).start()

    def out_5(chunk):
        for half in range(2):
            part = parts[chunk, half, 0, 0]
            for way in range(2):
                out_copy(chunk, half, way, 3).wait_recv()
                part = part + rv4[chunk, half, way].astype(F32)
            start = chunk * T + half * 128
            out_ref[start : start + 128] = part.astype(BF16)

    def late(m):
        place_of = m + div(m + 14, 15) + div(m, 15)
        chunk = rem(place_of, 2)
        return chunk, div(place_of - 3 * chunk, 2)

    def send_first(chunk, block):
        for head in range(2):
            send_part(chunk, block, head, 0, head)

    def pass_on(chunk, block, step, way):
        for head in range(2):
            have = jnp.logical_or(step > 1, way == head)
            pl.when(have)(lambda head=head: merge_part(chunk, block, way, step - 1, head))
            send_part(chunk, block, way, step, head)

    def complete(chunk, block):
        for head in range(2):
            rows = pl.ds(head * HD, HD)
            for way in range(2):
                merge_part(chunk, block, way, 3, head)
            done = blocks_o[block, rows, :] / blocks_s[block, pl.ds(2 * head + 1, 1), :]
            attb[chunk, :, rows] = done.T.astype(BF16)

    def return_block(m):
        chunk, i = late(m)
        block = chunk * 8 + i
        step, way, _ = sides(i)
        pl.when(i == 0)(lambda: send_first(chunk, block))
        pl.when(jnp.logical_and(i > 0, i < 7))(lambda: pass_on(chunk, block, step, way))
        pl.when(i == 7)(lambda: complete(chunk, block))

    def gain_finish():
        for stage in range(2):
            for d in (1, 2, 3):
                gain_copy(stage, d).wait_send()

    def one_block(m, carry):
        def number(m):
            chunk, i = late(m)
            return chunk * 8 + i

        now, later = number(m), number(rem(m + 1, 16))
        phase(now, 0, now, 1)
        phase(now, 1, later, 0)
        pl.when(m > 0)(lambda: return_block(m - 1))
        pl.when(m == 14)(lambda: out_1(0))
        for at, work in (
            (2, gather_a.finish),
            (3, gather_b.finish),
            (4, gather_e.finish),
            (5, ring_a.finish),
            (6, ring_b.finish),
            (7, gain_finish),
        ):
            pl.when(m == at)(work)
        return carry

    phase(None, 0, 0, 0)
    lax.fori_loop(0, 8 * CHUNKS, one_block, 0)
    out_2(0)
    complete(1, 15)
    out_1(1)
    out_3(0)
    out_2(1)
    out_4(0)
    out_3(1)
    out_5(0)
    out_4(1)
    out_5(1)

    for chunk in range(CHUNKS):
        for way in range(2):
            for step in range(4):
                for half in range(2):
                    if step > 0 or half == way:
                        o_copy(chunk, way, step, half).wait_send()
                    for db in range(4 if step < 2 else 1):
                        out_copy(chunk, half, way, step, db).wait_send()


def per_device(hidden_in, norm_gain, w_query, enc_states, w_key, w_value, w_out, block_counts):
    any_spec = pl.BlockSpec(memory_space=pl.ANY)
    vmem = pltpu.VMEM
    dma = pltpu.SemaphoreType.DMA
    scratch = [
        vmem((HEAD * F, F), BF16),
        vmem((DE, F), BF16),
        vmem((DE, F), BF16),
        vmem((F, HEAD * F), BF16),
        vmem((CHUNKS, HEAD, T, F), BF16),
        vmem((HEAD, BLOCK, DE), BF16),
        vmem((CHUNKS, Z, F, T), BF16),
        vmem((2, KEYS, HD), BF16),
        vmem((F, KEYS), BF16),
        vmem((KEYS, T), F32),
        vmem((KEYS, T), F32),
        vmem((8, T), F32),
        vmem((8, T), F32),
        vmem((CHUNKS * Z, F, T), F32),
        vmem((CHUNKS * Z, 8, T), F32),
        vmem((SLOTS, 8, T), F32),
        vmem((CHUNKS, 2, 4, 2, HD + 16, T), BF16),
        vmem((CHUNKS, 2, 4, 2, HD + 16, T), BF16),
        vmem((CHUNKS, T, F), BF16),
        vmem((CHUNKS, 2, 2, 4, 64, F), BF16),
        vmem((CHUNKS, 2, 2, 4, 64, F), BF16),
        vmem((CHUNKS, 2, 2, 4, 128, F), BF16),
        vmem((CHUNKS, 2, 2, 4, 128, F), BF16),
        vmem((CHUNKS, 2, 2, 64, F), BF16),
        vmem((CHUNKS, 2, 2, 64, F), BF16),
        vmem((CHUNKS, 2, 2, 128, F), BF16),
        vmem((CHUNKS, 2, 2, 128, F), BF16),
        vmem((CHUNKS, 2, 4, 4, 128, F), F32),
        vmem((HEAD, 8, F), F32),
        dma((7,)),
        dma((6,)),
        dma((6,)),
        dma((3, 40)),
        dma((3, 40)),
        dma((CHUNKS * 16,)),
        dma((CHUNKS * 16,)),
        dma((CHUNKS * 16,)),
        dma((CHUNKS * 16,)),
        dma((CHUNKS * 40,)),
        dma((CHUNKS * 40,)),
    ]
    return pl.pallas_call(
        kernel,
        out_shape=jax.ShapeDtypeStruct((CHUNKS * T, F), BF16),
        in_specs=[
            any_spec,
            pl.BlockSpec(memory_space=pltpu.VMEM),
            any_spec,
            any_spec,
            any_spec,
            any_spec,
            any_spec,
            pl.BlockSpec(memory_space=pltpu.SMEM),
        ],
        out_specs=pl.BlockSpec(memory_space=pltpu.VMEM),
        scratch_shapes=scratch,
        compiler_params=pltpu.CompilerParams(
            collective_id=0, has_side_effects=True, vmem_limit_bytes=60 * 1024 * 1024
        ),
        cost_estimate=pl.CostEstimate(
            flops=13_000_000_000, bytes_accessed=8_000_000, transcendentals=17_000_000
        ),
    )(
        hidden_in, norm_gain, w_query, enc_states, w_key, w_value, w_out, block_counts
    )


def solution(mesh):
    placed = (
        P(("dp", "span"), "head"),
        P("head"),
        P(None, "head"),
        P(("dp", "span", "head"), None),
        P(None, "head"),
        P(None, "head"),
        P("head", None),
        P("dp"),
    )
    return jax.shard_map(
        per_device, mesh=mesh, in_specs=placed, out_specs=P(("dp", "span"), "head"), check_vma=False
    )
```

time: 145 us -> 124 us (0.86)
  Pallas kernels: 142 us -> 122 us
    pallas_call x1, Pallas kernels: 142 us -> 122 us  [per_device(): pl.pallas_call(kernel, out_shape=jax.ShapeDtypeStruct((CHUNKS * T, F), BF...]
where the time goes in v2:
time: 124 us; the launch traced here: 123 us
  Pallas kernels  122 us (98%)
  local copies, waits for them, and re-layouts  1.67 us (1%)
    pallas_call x1, Pallas kernels, per_device(): pl.pallas_call(kernel, out_shape=jax.ShapeDtypeStruct((CHUNKS * T, F), BF...  122 us

profile of v2, /device:TPU:2, one launch (start us, length us, event | category | flops | bytes accessed | tf_op | source)
XLA Modules:
  0.0 123.3 jit_solution(2737264288118277498)
XLA Ops:
  0.0 121.6 %shard_map.82 = bf16[512,256]{1,0:T(8,128)(2,1)} custom-call(bf16[512,256]{1,0:T(8,128)(2,1)} %hidden_hbm.1, bf16[256]{0:T(256)(128)(2,1)} %gain_ref.1, bf16[4096,256]{1,0:T(8,128)(2,1)} %wq_hbm.1, bf16[128,1024]{1,0:T(8,128)(2,1)} %enc_hbm.1, bf16[1024,256]{1,0:T(8,128)(2,1)} %wk_hbm.1, bf16[1024,256]{1,0:T(8,128)(2,1)} %wv_hbm.1, ...), custom_call_target="tpu_custom_call" | custom-call | flops 12999999488 | bytes 8000000 | tf_op jit(solution)/shard_map/pallas_call | solution.py:659
  121.6 1.7 %copy.10 = bf16[512,256]{1,0:T(8,128)(2,1)} copy(bf16[512,256]{1,0:T(8,128)(2,1)} %shard_map.82) | data formatting | bytes 524288

commit v3 on v2

--- a/solution.py
+++ b/solution.py
@@ -19,6 +19,7 @@
 SLOTS = 16
 KEYS = BLOCK * SLOTS
 TILE = 256
+LAG = 0
 DE = 1024
 LOG2E = 1.4426950408889634
 COEF = LOG2E / math.sqrt(HD)
@@ -209,7 +210,7 @@
     wq, wk, wv, wo, nbuf, ebuf, qbuf, kbuf, vbuf, score_0, score_1, best_0, best_1, blocks_o, blocks_s, live_buf,
 
     osend, orecv, attb,
-    st1, rv1, st2, rv2, st3, rv3, st4, rv4, parts, gains,
+    st1, rv1, st2, rv2, st3, rv3, parts, gains,
     local_sem, ms_ss, ms_rs, ag_ss, ag_rs, q_ss, q_rs, o_ss, o_rs, x_ss, x_rs,
 ):
     place = Place()
@@ -444,13 +445,15 @@
         return (da, db) if half == 0 else (db, da)
 
     def out_copy(chunk, half, way, step, db=0):
-        send, recv = ((st1, rv1), (st2, rv2), (st3, rv3), (st4, rv4))[step]
-        off = 1 - 2 * way
-        to = place.at_xy(*out_axes(half, off, 0) if step < 2 else out_axes(half, 0, off))
-        index = ((chunk * 2 + half) * 2 + way) * 10 + (step * 4 + db if step < 2 else 6 + step)
-        source, target = send.at[chunk, half, way], recv.at[chunk, half, way]
         if step < 2:
-            source, target = source.at[db], target.at[db]
+            send, recv = ((st1, rv1), (st2, rv2))[step]
+            source, target = send.at[chunk, half, way, db], recv.at[chunk, half, way, db]
+            to = place.at_xy(*out_axes(half, 1 - 2 * way, 0))
+            index = ((chunk * 2 + half) * 2 + way) * 8 + step * 4 + db
+        else:
+            source, target = st3.at[chunk, half, db - 1], rv3.at[chunk, half, db - 1]
+            to = place.at_xy(*out_axes(half, 0, db))
+            index = CHUNKS * 32 + (chunk * 2 + half) * 3 + db - 1
         return pltpu.make_async_remote_copy(
             src_ref=source,
             dst_ref=target,
@@ -502,64 +505,49 @@
                 for way in range(2):
                     out_copy(chunk, half, way, 1, db).wait_recv()
                     part = part + rv2[chunk, half, way, db].astype(F32)
-                if db == 2:
-                    for way in range(2):
-                        st3[chunk, half, way] = part[64 * way : 64 * way + 64].astype(BF16)
-                        out_copy(chunk, half, way, 2).start()
+                if db > 0:
+                    st3[chunk, half, db - 1] = part.astype(BF16)
+                    out_copy(chunk, half, 0, 2, db).start()
                 else:
-                    parts[chunk, half, 0, db] = part
+                    parts[chunk, half, 0, 0] = part
 
     def out_4(chunk):
         for half in range(2):
-            for way in range(2):
-                same = slice(64 * way, 64 * way + 64)
-                rest = slice(64 - 64 * way, 128 - 64 * way)
-                db = (1, 3)[way]
-                st4[chunk, half, way, rest] = parts[chunk, half, 0, db, rest].astype(BF16)
-                out_copy(chunk, half, way, 2).wait_recv()
-                part = parts[chunk, half, 0, db, same] + rv3[chunk, half, way].astype(F32)
-                st4[chunk, half, way, same] = part.astype(BF16)
-                out_copy(chunk, half, way, 3).start()
-
-    def out_5(chunk):
-        for half in range(2):
             part = parts[chunk, half, 0, 0]
-            for way in range(2):
-                out_copy(chunk, half, way, 3).wait_recv()
-                part = part + rv4[chunk, half, way].astype(F32)
+            for db in (1, 3, 2):
+                out_copy(chunk, half, 0, 2, db).wait_recv()
+                part = part + rv3[chunk, half, db - 1].astype(F32)
             start = chunk * T + half * 128
             out_ref[start : start + 128] = part.astype(BF16)
 
     def late(m):
-        place_of = m + div(m + 14, 15) + div(m, 15)
-        chunk = rem(place_of, 2)
-        return chunk, div(place_of - 3 * chunk, 2)
-
-    def send_first(chunk, block):
-        for head in range(2):
-            send_part(chunk, block, head, 0, head)
-
-    def pass_on(chunk, block, step, way):
-        for head in range(2):
-            have = jnp.logical_or(step > 1, way == head)
-            pl.when(have)(lambda head=head: merge_part(chunk, block, way, step - 1, head))
-            send_part(chunk, block, way, step, head)
-
-    def complete(chunk, block):
-        for head in range(2):
-            rows = pl.ds(head * HD, HD)
-            for way in range(2):
-                merge_part(chunk, block, way, 3, head)
-            done = blocks_o[block, rows, :] / blocks_s[block, pl.ds(2 * head + 1, 1), :]
-            attb[chunk, :, rows] = done.T.astype(BF16)
-
-    def return_block(m):
+        begun = div(m + 16 - LAG, 16)
+        ending = div(m + LAG, 16)
+        both = begun * (1 - ending)
+        k = m - LAG + 16
+        odd = rem(k, 2)
+        i = (1 - begun) * m + both * (div(k, 2) - 8 + LAG * (1 - odd)) + ending * (m - 8)
+        return both * odd + ending, i
+
+    def pass_on(chunk, block, step, way, head):
+        have = jnp.logical_or(step > 1, way == head)
+        pl.when(have)(lambda: merge_part(chunk, block, way, step - 1, head))
+        send_part(chunk, block, way, step, head)
+
+    def complete(chunk, block, head):
+        rows = pl.ds(head * HD, HD)
+        for way in range(2):
+            merge_part(chunk, block, way, 3, head)
+        done = blocks_o[block, rows, :] / blocks_s[block, pl.ds(2 * head + 1, 1), :]
+        attb[chunk, :, rows] = done.T.astype(BF16)
+
+    def return_part(m, head):
         chunk, i = late(m)
         block = chunk * 8 + i
         step, way, _ = sides(i)
-        pl.when(i == 0)(lambda: send_first(chunk, block))
-        pl.when(jnp.logical_and(i > 0, i < 7))(lambda: pass_on(chunk, block, step, way))
-        pl.when(i == 7)(lambda: complete(chunk, block))
+        inner = jnp.logical_and(i > 0, i < 7)
+        pl.when(inner)(lambda: pass_on(chunk, block, step, way, head))
+        pl.when(i == 7)(lambda: complete(chunk, block, head))
 
     def gain_finish():
         for stage in range(2):
@@ -573,9 +561,12 @@
 
         now, later = number(m), number(rem(m + 1, 16))
         phase(now, 0, now, 1)
+        pl.when(rem(now, 8) == 0)(lambda: send_part(div(now, 8), now, 0, 0, 0))
+        pl.when(m > 0)(lambda: return_part(m - 1, 0))
         phase(now, 1, later, 0)
-        pl.when(m > 0)(lambda: return_block(m - 1))
-        pl.when(m == 14)(lambda: out_1(0))
+        pl.when(rem(now, 8) == 0)(lambda: send_part(div(now, 8), now, 1, 0, 1))
+        pl.when(m > 0)(lambda: return_part(m - 1, 1))
+        pl.when(m == 15)(lambda: out_1(0))
         for at, work in (
             (2, gather_a.finish),
             (3, gather_b.finish),
@@ -589,16 +580,15 @@
 
     phase(None, 0, 0, 0)
     lax.fori_loop(0, 8 * CHUNKS, one_block, 0)
+    for head in range(2):
+        complete(1, 15, head)
+    out_1(1)
     out_2(0)
-    complete(1, 15)
-    out_1(1)
+    out_2(1)
     out_3(0)
-    out_2(1)
+    out_3(1)
     out_4(0)
-    out_3(1)
-    out_5(0)
     out_4(1)
-    out_5(1)
 
     for chunk in range(CHUNKS):
         for way in range(2):
@@ -606,8 +596,9 @@
                 for half in range(2):
                     if step > 0 or half == way:
                         o_copy(chunk, way, step, half).wait_send()
-                    for db in range(4 if step < 2 else 1):
-                        out_copy(chunk, half, way, step, db).wait_send()
+                    for db in range(4):
+                        if step < 2 or (step == 2 and way == 0 and db > 0):
+                            out_copy(chunk, half, way, step, db).wait_send()
 
 
 def per_device(hidden_in, norm_gain, w_query, enc_states, w_key, w_value, w_out, block_counts):
@@ -638,10 +629,8 @@
         vmem((CHUNKS, 2, 2, 4, 64, F), BF16),
         vmem((CHUNKS, 2, 2, 4, 128, F), BF16),
         vmem((CHUNKS, 2, 2, 4, 128, F), BF16),
-        vmem((CHUNKS, 2, 2, 64, F), BF16),
-        vmem((CHUNKS, 2, 2, 64, F), BF16),
-        vmem((CHUNKS, 2, 2, 128, F), BF16),
-        vmem((CHUNKS, 2, 2, 128, F), BF16),
+        vmem((CHUNKS, 2, 3, 128, F), BF16),
+        vmem((CHUNKS, 2, 3, 128, F), BF16),
         vmem((CHUNKS, 2, 4, 4, 128, F), F32),
         vmem((HEAD, 8, F), F32),
         dma((7,)),
@@ -653,8 +642,8 @@
         dma((CHUNKS * 16,)),
         dma((CHUNKS * 16,)),
         dma((CHUNKS * 16,)),
-        dma((CHUNKS * 40,)),
-        dma((CHUNKS * 40,)),
+        dma((CHUNKS * 38,)),
+        dma((CHUNKS * 38,)),
     ]
     return pl.pallas_call(
         kernel,

time: 124 us -> 117 us (0.944)
  Pallas kernels: 122 us -> 114 us
    pallas_call x1, Pallas kernels: 122 us -> 114 us  [per_device(): pl.pallas_call(kernel, out_shape=jax.ShapeDtypeStruct((CHUNKS * T, F), BF...]
where the time goes in v3:
time: 117 us; the launch traced here: 116 us
  Pallas kernels  114 us (97%)
  local copies, waits for them, and re-layouts  1.67 us (1%)
    pallas_call x1, Pallas kernels, per_device(): pl.pallas_call(kernel, out_shape=jax.ShapeDtypeStruct((CHUNKS * T, F), BF...  114 us

profile of v3, /device:TPU:2, one launch (start us, length us, event | category | flops | bytes accessed | tf_op | source)
XLA Modules:
  0.0 116.2 jit_solution(7622499932610053243)
XLA Ops:
  0.0 114.5 %shard_map.82 = bf16[512,256]{1,0:T(8,128)(2,1)} custom-call(bf16[512,256]{1,0:T(8,128)(2,1)} %hidden_hbm.1, bf16[256]{0:T(256)(128)(2,1)} %gain_ref.1, bf16[4096,256]{1,0:T(8,128)(2,1)} %wq_hbm.1, bf16[128,1024]{1,0:T(8,128)(2,1)} %enc_hbm.1, bf16[1024,256]{1,0:T(8,128)(2,1)} %wk_hbm.1, bf16[1024,256]{1,0:T(8,128)(2,1)} %wv_hbm.1, ...), custom_call_target="tpu_custom_call" | custom-call | flops 12999999488 | bytes 8000000 | tf_op jit(solution)/shard_map/pallas_call | solution.py:648
  114.5 1.7 %copy.10 = bf16[512,256]{1,0:T(8,128)(2,1)} copy(bf16[512,256]{1,0:T(8,128)(2,1)} %shard_map.82) | data formatting | bytes 524288

commit v4 on v3

--- a/solution.py
+++ b/solution.py
@@ -19,7 +19,8 @@
 SLOTS = 16
 KEYS = BLOCK * SLOTS
 TILE = 256
-LAG = 0
+FIRST = 0
+BLOCK_ORDER = (0, 1, 2, 8, 9, 10, 3, 4, 11, 12, 5, 6, 13, 14, 7, 15)
 DE = 1024
 LOG2E = 1.4426950408889634
 COEF = LOG2E / math.sqrt(HD)
@@ -237,7 +238,7 @@
     barrier = pltpu.get_barrier_semaphore()
     partners = [place.at_xy(d, 0) for d in (1, 2, 3)]
     partners += [place.at_xy(0, d) for d in (1, 2, 3)]
-    partners += [place.at_z(1), place.at_z(-1)]
+    partners += [place.at_z(d) for d in (1, -1, 2, -2)]
     for partner in partners:
         pl.semaphore_signal(barrier, inc=1, device_id=partner, device_id_type=MESH)
 
@@ -410,36 +411,35 @@
             dst_ref=orecv.at[chunk, way, step, head],
             send_sem=o_ss.at[index],
             recv_sem=o_rs.at[index],
-            device_id=(place.dp, wrap(z + 1 - 2 * way, Z), place.head),
+            device_id=(place.dp, wrap(z + (1 - 2 * way) * (2 if step is FIRST else 1), Z), place.head),
             device_id_type=MESH,
         )
 
-    def send_part(chunk, block, way, step, head):
-        osend[chunk, way, step, head, :HD] = blocks_o[block, pl.ds(head * HD, HD), :].astype(BF16)
-        rows = split3(blocks_s[block, pl.ds(2 * head, 1), :])
-        rows += split3(blocks_s[block, pl.ds(2 * head + 1, 1), :])
-        rows = jnp.concatenate(rows + [jnp.zeros((10, T), F32)], axis=0)
-        osend[chunk, way, step, head, HD:] = rows.astype(BF16)
+    def held(block, head):
+        return (
+            blocks_o[block, pl.ds(head * HD, HD), :],
+            blocks_s[block, pl.ds(2 * head, 1), :],
+            blocks_s[block, pl.ds(2 * head + 1, 1), :],
+        )
+
+    def send_part(chunk, way, step, head, part):
+        values, best, total = part
+        osend[chunk, way, step, head, :HD] = values.astype(BF16)
+        rows = split3(best) + split3(total) + [jnp.zeros((10, T), F32)]
+        osend[chunk, way, step, head, HD:] = jnp.concatenate(rows, axis=0).astype(BF16)
         o_copy(chunk, way, step, head).start()
 
-    def merge_part(chunk, block, way, step, head):
+    def merge_part(chunk, way, step, head, part):
         o_copy(chunk, way, step, head).wait_recv()
-        rows = pl.ds(head * HD, HD)
-        best_row = pl.ds(2 * head, 1)
-        sum_row = pl.ds(2 * head + 1, 1)
+        values, best_a, total = part
         stats = orecv[chunk, way, step, head, HD:, :].astype(F32)
-        best_a = blocks_s[block, best_row, :]
         best_b = stats[0:1] + stats[1:2] + stats[2:3]
-        sum_b = stats[3:4] + stats[4:5] + stats[5:6]
+        total_b = stats[3:4] + stats[4:5] + stats[5:6]
         best = jnp.maximum(best_a, best_b)
         scale_a = jnp.exp2(best_a - best)
         scale_b = jnp.exp2(best_b - best)
-        blocks_s[block, best_row] = best
-        blocks_s[block, sum_row] = blocks_s[block, sum_row, :] * scale_a + sum_b * scale_b
-        blocks_o[block, rows] = (
-            blocks_o[block, rows, :] * scale_a
-            + orecv[chunk, way, step, head, :HD, :].astype(F32) * scale_b
-        )
+        values = values * scale_a + orecv[chunk, way, step, head, :HD, :].astype(F32) * scale_b
+        return values, best, total * scale_a + total_b * scale_b
 
     def out_axes(half, da, db):
         return (da, db) if half == 0 else (db, da)
@@ -520,32 +520,45 @@
             start = chunk * T + half * 128
             out_ref[start : start + 128] = part.astype(BF16)
 
-    def late(m):
-        begun = div(m + 16 - LAG, 16)
-        ending = div(m + LAG, 16)
-        both = begun * (1 - ending)
-        k = m - LAG + 16
-        odd = rem(k, 2)
-        i = (1 - begun) * m + both * (div(k, 2) - 8 + LAG * (1 - odd)) + ending * (m - 8)
-        return both * odd + ending, i
+    def number(m):
+        block = BLOCK_ORDER[0]
+        for at in range(1, 16):
+            block = block + div(m + 16 - at, 16) * (BLOCK_ORDER[at] - BLOCK_ORDER[at - 1])
+        return block
+
+    def send_first(block, head):
+        i = rem(block, 8)
+        chunk = div(block, 8)
+        pl.when(i == 0)(lambda: send_part(chunk, head, FIRST, head, held(block, head)))
+        pl.when(jnp.logical_and(i > 0, i < 3))(
+            lambda: send_part(chunk, rem(i + 1, 2), 1, head, held(block, head))
+        )
 
     def pass_on(chunk, block, step, way, head):
-        have = jnp.logical_or(step > 1, way == head)
-        pl.when(have)(lambda: merge_part(chunk, block, way, step - 1, head))
-        send_part(chunk, block, way, step, head)
+        both = jnp.logical_and(step == 2, way == head)
+
+        @pl.when(both)
+        def _():
+            part = merge_part(chunk, way, FIRST, head, held(block, head))
+            part = merge_part(chunk, way, 1, head, part)
+            send_part(chunk, way, 2, head, part)
+
+        @pl.when(jnp.logical_not(both))
+        def _():
+            part = merge_part(chunk, way, step - 1, head, held(block, head))
+            send_part(chunk, way, step, head, part)
 
     def complete(chunk, block, head):
-        rows = pl.ds(head * HD, HD)
+        part = held(block, head)
         for way in range(2):
-            merge_part(chunk, block, way, 3, head)
-        done = blocks_o[block, rows, :] / blocks_s[block, pl.ds(2 * head + 1, 1), :]
-        attb[chunk, :, rows] = done.T.astype(BF16)
+            part = merge_part(chunk, way, 3, head, part)
+        attb[chunk, :, pl.ds(head * HD, HD)] = (part[0] / part[2]).T.astype(BF16)
 
     def return_part(m, head):
-        chunk, i = late(m)
-        block = chunk * 8 + i
+        block = number(m)
+        chunk, i = div(block, 8), rem(block, 8)
         step, way, _ = sides(i)
-        inner = jnp.logical_and(i > 0, i < 7)
+        inner = jnp.logical_and(i > 2, i < 7)
         pl.when(inner)(lambda: pass_on(chunk, block, step, way, head))
         pl.when(i == 7)(lambda: complete(chunk, block, head))
 
@@ -555,16 +568,12 @@
                 gain_copy(stage, d).wait_send()
 
     def one_block(m, carry):
-        def number(m):
-            chunk, i = late(m)
-            return chunk * 8 + i
-
         now, later = number(m), number(rem(m + 1, 16))
         phase(now, 0, now, 1)
-        pl.when(rem(now, 8) == 0)(lambda: send_part(div(now, 8), now, 0, 0, 0))
+        send_first(now, 0)
         pl.when(m > 0)(lambda: return_part(m - 1, 0))
         phase(now, 1, later, 0)
-        pl.when(rem(now, 8) == 0)(lambda: send_part(div(now, 8), now, 1, 0, 1))
+        send_first(now, 1)
         pl.when(m > 0)(lambda: return_part(m - 1, 1))
         pl.when(m == 15)(lambda: out_1(0))
         for at, work in (
@@ -647,7 +656,7 @@
     ]
     return pl.pallas_call(
         kernel,
-        out_shape=jax.ShapeDtypeStruct((CHUNKS * T, F), BF16),
+        out_shape=pltpu.VMEM((CHUNKS * T, F), BF16),
         in_specs=[
             any_spec,
             pl.BlockSpec(memory_space=pltpu.VMEM),

time: 117 us -> 115 us (0.983)
  no operation moved by 1% of the time
where the time goes in v4:
time: 115 us
  Pallas kernels  114 us (99%)
    pallas_call x1, Pallas kernels, per_device(): pl.pallas_call(kernel, out_shape=pltpu.VMEM((CHUNKS * T, F), BF16), in_sp...  114 us

profile of v4, /device:TPU:2, one launch (start us, length us, event | category | flops | bytes accessed | tf_op | source)
XLA Modules:
  0.0 114.5 jit_solution(13826802380634381679)
XLA Ops:
  0.0 113.8 %shard_map.82 = bf16[512,256]{1,0:T(8,128)(2,1)S(1)} custom-call(bf16[512,256]{1,0:T(8,128)(2,1)} %hidden_hbm.1, bf16[256]{0:T(256)(128)(2,1)} %gain_ref.1, bf16[4096,256]{1,0:T(8,128)(2,1)} %wq_hbm.1, bf16[128,1024]{1,0:T(8,128)(2,1)} %enc_hbm.1, bf16[1024,256]{1,0:T(8,128)(2,1)} %wk_hbm.1, bf16[1024,256]{1,0:T(8,128)(2,1)} %wv_hbm.1, ...), custom_call_target="tpu_custom_call" | custom-call | flops 12999999488 | bytes 8000000 | tf_op jit(solution)/shard_map/pallas_call | solution.py:657
  113.8 0.7 copy.10

commit v5 on v4

--- a/solution.py
+++ b/solution.py
@@ -480,6 +480,7 @@
                 for way in range(2):
                     st1[chunk, half, way, db] = part[64 * way : 64 * way + 64]
                     out_copy(chunk, half, way, 0, db).start()
+    def out_rest(chunk):
         for da in (1, 3, 0):
             for db in ORDER:
                 for half in range(2):
@@ -576,6 +577,7 @@
         send_first(now, 1)
         pl.when(m > 0)(lambda: return_part(m - 1, 1))
         pl.when(m == 15)(lambda: out_1(0))
+        pl.when(m == 15)(lambda: out_rest(0))
         for at, work in (
             (2, gather_a.finish),
             (3, gather_b.finish),
@@ -593,6 +595,7 @@
         complete(1, 15, head)
     out_1(1)
     out_2(0)
+    out_rest(1)
     out_2(1)
     out_3(0)
     out_3(1)

time: 115 us -> 114 us (level)
  no operation moved by 1% of the time
where the time goes in v5:
time: 114 us
  Pallas kernels  113 us (99%)
    pallas_call x1, Pallas kernels, per_device(): pl.pallas_call(kernel, out_shape=pltpu.VMEM((CHUNKS * T, F), BF16), in_sp...  113 us

profile of v5, /device:TPU:2, one launch (start us, length us, event | category | flops | bytes accessed | tf_op | source)
XLA Modules:
  0.0 114.1 jit_solution(9153328592608515383)
XLA Ops:
  0.0 113.4 %shard_map.82 = bf16[512,256]{1,0:T(8,128)(2,1)S(1)} custom-call(bf16[512,256]{1,0:T(8,128)(2,1)} %hidden_hbm.1, bf16[256]{0:T(256)(128)(2,1)} %gain_ref.1, bf16[4096,256]{1,0:T(8,128)(2,1)} %wq_hbm.1, bf16[128,1024]{1,0:T(8,128)(2,1)} %enc_hbm.1, bf16[1024,256]{1,0:T(8,128)(2,1)} %wk_hbm.1, bf16[1024,256]{1,0:T(8,128)(2,1)} %wv_hbm.1, ...), custom_call_target="tpu_custom_call" | custom-call | flops 12999999488 | bytes 8000000 | tf_op jit(solution)/shard_map/pallas_call | solution.py:660
  113.4 0.7 copy.10
